TPU v7x, 32 devices: a whole 2x2x4 slice. The times are simulated.
32 devices in a mesh: row: 8 (over z, x), col: 4 (over y, core).
Axes of the slice: x: 2, y: 2, z: 4, core: 2. Of those that a mesh axis runs over, the one named last changes fastest.
Arguments:
- amplitudes: bfloat16 [4096, 2048], P('row', 'col'), may hold values from -6 to 6
- integrals: bfloat16 [2048, 2048], P('col', 'row'), may hold values from -0.1875 to 0.1875
- base_residual: float32 [4096, 2048], P('row', 'col'), may hold values from -6 to 6
- inv_denominators: float32 [4096, 2048], P('row', 'col'), may hold values from 0.1 to 0.5
- amp_mask: int32 [16, 8], P('row', 'col'), may hold values 0 or 1
- int_mask: int32 [8, 8], P('col', 'row'), may hold values 0 or 1
- res_mask: int32 [16, 8], P('row', 'col'), may hold values 0 or 1
Outputs:
- new_amplitudes: bfloat16 [4096, 2048], P('row', 'col')
- residual: float32 [4096, 2048], P('row', 'col')
Inputs may be any that keep to these rules, and one draw needn't show every extreme that they name: `amp_mask`: tile kept (1) or dropped (0). `int_mask`: tile kept (1) or dropped (0). `res_mask`: tile kept (1) or dropped (0).
All inputs are finite; a program needn't handle non-finite values. No bound on the sum of `amp_mask` or of `int_mask` or of `res_mask` on one device may be relied on, other than what follows from the above.
Results may differ from a plain program's by a relative error of at most 0.012.
Values may be sent and summed in bfloat16 or wider, within the bound.
A program may use at most 128 MiB of HBM per device.

v0:
```python
import jax
import jax.numpy as jnp
from jax import lax
from jax.sharding import PartitionSpec as P

ITERS = 2


def expand(block, mask):
    tile_rows, tile_cols = mask.shape
    rows, cols = block.shape
    shaped = block.reshape(tile_rows, rows // tile_rows, tile_cols, cols // tile_cols)
    return (shaped * mask[:, None, :, None].astype(block.dtype)).reshape(rows, cols)


def shards(amplitudes, integrals, base_residual, inv_denominators, amp_mask, int_mask, res_mask):
    masked_ints = expand(integrals, int_mask)
    ints_all = lax.all_gather(masked_ints, "row", axis=1, tiled=True)
    amps = amplitudes
    residual = base_residual
    for step in range(ITERS):
        masked_amps = expand(amps, amp_mask)
        term = jnp.dot(masked_amps, ints_all, preferred_element_type=jnp.float32)
        ladder = lax.psum_scatter(
            term.astype(jnp.bfloat16), "col", scatter_dimension=1, tiled=True
        ).astype(jnp.float32)
        residual = expand(base_residual + ladder, res_mask)
        amps = (amps.astype(jnp.float32) - inv_denominators * residual).astype(jnp.bfloat16)
    return (amps, residual)


def solution(mesh):
    in_specs = (
        P("row", "col"),
        P("col", "row"),
        P("row", "col"),
        P("row", "col"),
        P("row", "col"),
        P("col", "row"),
        P("row", "col"),
    )
    out_specs = (P("row", "col"), P("row", "col"))
    return jax.shard_map(shards, mesh=mesh, in_specs=in_specs, out_specs=out_specs, check_vma=False)
```

profile of v0, /device:TPU:0, one launch (start us, length us, event | category | flops | bytes accessed | tf_op | source)
XLA Modules:
  0.0 144.6 jit_solution(5935986830572258552)
XLA Ops:
  7.2 0.0 copy-start.3
  7.2 0.0 all-gather.2.cloned.1.call-start
  7.2 0.7 convert_bitcast_fusion
  7.9 0.1 broadcast_bitcast_fusion
  8.0 1.8 %broadcast_multiply_fusion = bf16[512,256]{1,0:T(8,128)(2,1)} fusion(bf16[512,256]{1,0:T(8,128)(2,1)} %param.8, bf16[512]{0:T(512)(128)(2,1)S(1)} %bitcast.19), kind=kLoop, calls=%fused_computation.7 | loop fusion | flops 131072 | bytes 525312 | tf_op jit(solution)/shard_map/mul | solution.py:13
  9.8 0.0 all-gather.2.cloned.1.call-update
  9.8 0.0 reduce-scatter.3.cloned.1.call-start
  9.9 0.7 convert_element_type.46
  10.6 0.3 mul.57
  10.9 0.1 copy.9
  11.0 0.0 copy-start.4
  11.0 53.4 %all-gather.2.cloned.1.call-done = bf16[512,2048]{1,0:T(8,128)(2,1)} async-done(((bf16[512,256]{1,0:T(8,128)(2,1)}), bf16[512,2048]{1,0:T(8,128)(2,1)}) %all-gather.2.cloned.1.call-update) | async-done | bytes 2097168 | tf_op jit(solution)/shard_map/all_gather | solution.py:18
  64.4 0.0 copy-done.3
  64.4 4.2 %convolution_convert_fusion.1 = bf16[512,2048]{1,0:T(8,128)(2,1)} fusion(bf16[512,2048]{1,0:T(8,128)(2,1)} %all-gather.2.cloned.1.call-done, bf16[512,512]{1,0:T(8,128)(2,1)S(1)} %copy-done.3, bf16[512,512]{1,0:T(8,128)(2,1)S(1)} %bitcast.17), kind=kOutput, calls=%fused_computation.1 | convolution fusion | flops 1075052544 | bytes 5242880 | tf_op jit(solution)/shard_map/dot_general | solution.py:23
  68.6 0.0 copy-done.4
  68.6 0.0 reduce-scatter.3.cloned.1.call-update
  68.6 0.0 copy-start
  68.6 0.0 copy-start.1
  68.7 0.0 reduce-scatter.5.cloned.1.call-start
  68.7 0.6 copy-done.6
  69.3 0.3 mul.64
  69.6 0.1 copy.11
  69.7 28.7 %reduce-scatter.3.cloned.1.call-done = bf16[512,512]{1,0:T(8,128)(2,1)} async-done(((bf16[512,2048]{1,0:T(8,128)(2,1)}), bf16[512,512]{1,0:T(8,128)(2,1)}) %reduce-scatter.3.cloned.1.call-update) | async-done | bytes 524304 | tf_op jit(solution)/shard_map/reduce_scatter | solution.py:24
  98.4 0.0 copy-done.1
  98.4 1.8 %subtract_convert_fusion.1 = bf16[512,512]{1,0:T(8,128)(2,1)S(1)} fusion(f32[512,512]{1,0:T(8,128)S(1)} %copy-done, f32[512,512]{1,0:T(8,128)S(1)} %bitcast.13, f32[512,512]{1,0:T(8,128)S(1)} %copy-done.1, bf16[512,512]{1,0:T(8,128)(2,1)} %reduce-scatter.3.cloned.1.call-done, bf16[512,512]{1,0:T(8,128)(2,1)} %param.7), kind=kLoop, calls=%fused_computation.4 | loop fusion | flops 1835008 | bytes 4718592 | tf_op jit(solution)/shard_map/convert_element_type | solution.py:28
  100.2 0.0 copy-start.2
  100.2 0.8 copy-done.2
  101.0 0.0 copy-done.7
  101.0 2.6 %convolution_convert_fusion = bf16[512,2048]{1,0:T(8,128)(2,1)} fusion(bf16[512,2048]{1,0:T(8,128)(2,1)S(1)} %copy-done.7, bf16[512,512]{1,0:T(8,128)(2,1)S(1)} %subtract_convert_fusion.1, bf16[512,512]{1,0:T(8,128)(2,1)S(1)} %bitcast.18), kind=kOutput, calls=%fused_computation | convolution fusion | flops 1075052544 | bytes 5242880 | tf_op jit(solution)/shard_map/dot_general | solution.py:23
  103.6 0.0 reduce-scatter.5.cloned.1.call-update
  103.6 31.6 %reduce-scatter.5.cloned.1.call-done = bf16[512,512]{1,0:T(8,128)(2,1)} async-done(((bf16[512,2048]{1,0:T(8,128)(2,1)}), bf16[512,512]{1,0:T(8,128)(2,1)}) %reduce-scatter.5.cloned.1.call-update) | async-done | bytes 524304 | tf_op jit(solution)/shard_map/reduce_scatter | solution.py:24
  135.3 2.8 %subtract_convert_fusion = (bf16[512,512]{1,0:T(8,128)(2,1)}, f32[512,512]{1,0:T(8,128)}) fusion(f32[512,512]{1,0:T(8,128)S(1)} %copy-done, bf16[512,512]{1,0:T(8,128)(2,1)} %copy-done.2, f32[512,512]{1,0:T(8,128)S(1)} %bitcast.14, f32[512,512]{1,0:T(8,128)S(1)} %copy-done.1, bf16[512,512]{1,0:T(8,128)(2,1)} %reduce-scatter.5.cloned.1.call-done), kind=kLoop, calls=%fused_computation.2 | loop fusion | flops 1835008 | bytes 5767168 | tf_op jit(solution)/shard_map/convert_element_type | solution.py:28
  (7 shorter events, 0.0 us)
Async XLA Ops:
  7.2 57.3 %copy-start.3 = (bf16[512,512]{1,0:T(8,128)(2,1)S(1)}, bf16[512,512]{1,0:T(8,128)(2,1)}, u32[]{:S(2)}) copy-start(bf16[512,512]{1,0:T(8,128)(2,1)} %param.7) | copy-start | bytes 1572868
  7.2 57.3 %all-gather.2.cloned.1.call-start = ((), (), s32[]{:S(2)}) async-start(), calls=%async_computation.2 | async-start | bytes 2359296 | tf_op jit(solution)/shard_map/all_gather | solution.py:18
  9.8 88.6 %reduce-scatter.3.cloned.1.call-start = ((), (), s32[]{:S(2)}) async-start(), calls=%async_computation.3 | async-start | bytes 2621440 | tf_op jit(solution)/shard_map/reduce_scatter | solution.py:24
  11.0 57.6 %copy-start.4 = (bf16[64,8,2,256]{3,1,2,0:T(8,128)(2,1)}, bf16[64,8,2,256]{3,1,2,0:T(8,128)(2,1)S(1)}, u32[]{:S(2)}) copy-start(bf16[64,8,2,256]{3,1,2,0:T(8,128)(2,1)S(1)} %copy.9) | copy-start | bytes 1572868
  68.6 0.7 copy-start.6
  68.6 29.8 %copy-start = (f32[512,512]{1,0:T(8,128)S(1)}, f32[512,512]{1,0:T(8,128)}, u32[]{:S(2)}) copy-start(f32[512,512]{1,0:T(8,128)} %param.10) | copy-start | bytes 3145732
  68.6 29.7 %copy-start.1 = (f32[512,512]{1,0:T(8,128)S(1)}, f32[512,512]{1,0:T(8,128)}, u32[]{:S(2)}) copy-start(f32[512,512]{1,0:T(8,128)} %param.9) | copy-start | bytes 3145732
  68.7 66.6 %reduce-scatter.5.cloned.1.call-start = ((), (), s32[]{:S(2)}) async-start(), calls=%async_computation.4 | async-start | bytes 2621440 | tf_op jit(solution)/shard_map/reduce_scatter | solution.py:24
  98.4 2.6 %copy-start.5 = (bf16[64,8,2,256]{3,1,2,0:T(8,128)(2,1)S(1)}, bf16[64,8,2,256]{3,1,2,0:T(8,128)(2,1)}, u32[]{:S(2)}) copy-start(bf16[64,8,2,256]{3,1,2,0:T(8,128)(2,1)} %copy-done.4) | copy-start | bytes 1572868
  98.4 2.6 %copy-start.7 = (bf16[512,2048]{1,0:T(8,128)(2,1)S(1)}, bf16[512,2048]{1,0:T(8,128)(2,1)}, u32[]{:S(2)}) copy-start(bf16[512,2048]{1,0:T(8,128)(2,1)} %all-gather.2.cloned.1.call-done) | copy-start | bytes 6291460
  100.2 0.8 copy-start.2
Sparse Core Ops, SparseCore 0:
  10.6 53.7 all-gather.1
  68.8 29.5 reduce-scatter.2
  103.8 31.4 reduce-scatter.4
where the time goes:
time: 145 us
  waiting for transfers between devices  114 us (79%)
  between operations  13.8 us (10%)
  other arithmetic  7.79 us (5%)
  matrix products  6.76 us (5%)
  local copies, waits for them, and re-layouts  2.32 us (2%)
    reduce_scatter x2, waiting for transfers between devices, shards(): lax.psum_scatter(term.astype(jnp.bfloat16), 'col', scatter_dimension=1, t...  60.3 us
    all_gather x1, waiting for transfers between devices, shards(): ints_all = lax.all_gather(masked_ints, 'row', axis=1, tiled=True)  53.4 us
    dot_general x2, matrix products, shards(): term = jnp.dot(masked_amps, ints_all, preferred_element_type=jnp.float32)  6.76 us
    convert_element_type x2, other arithmetic, shards(): (amps.astype(jnp.float32) - inv_denominators * residual).astype(jnp.bfloa...  4.61 us
  transfers between devices with their start and end apart: 3, of which 3 were waited for; matrix products, arithmetic and copies ran while one was open for 1% of the time, Pallas kernels for 0%

commit v1 on v0

v1 whole, which is shorter than its diff:
```python
import functools

import jax
import jax.numpy as jnp
from jax import lax
from jax.experimental import pallas as pl
from jax.experimental.pallas import tpu as pltpu
from jax.sharding import PartitionSpec as P

ITERS = 2
MESH = pl.DeviceIdType.MESH


def kernel(
    n_row, n_col,
    amp_mask, int_mask, res_mask, amps_hbm, ints_hbm, base_hbm, inv_hbm,
    new_hbm, res_hbm,
    raw, ints, amps, masked, base, inv, hold, pair_out, pair_in, far_out, far_in, res,
    load_sem, store_sem, up_sem, down_sem, across_sem, ints_sem,
    pair_send, pair_recv, far_send, far_recv,
):
    row, col = lax.axis_index("row"), lax.axis_index("col")
    z, x = row // 2, row % 2
    place, core = col // 2, col % 2
    n_z, n_place = n_row // 2, n_col // 2
    rows, width = amps.shape[0], ints.shape[2]
    pieces = amps.shape[1] // width

    loads = [
        pltpu.make_async_copy(src, dst, load_sem.at[i])
        for i, (src, dst) in enumerate(
            ((ints_hbm, raw), (amps_hbm, amps), (base_hbm, base), (inv_hbm, inv))
        )
    ]
    for load in loads:
        load.start()

    barrier = pltpu.get_barrier_semaphore()

    def greet(r, c):
        pl.semaphore_signal(barrier, inc=1, device_id=(r, c), device_id_type=MESH)

    greet(row, place * 2 + 1 - core)
    greet(z * 2 + 1 - x, col)

    @pl.when(z > 0)
    def _():
        greet(row - 2, col)

    @pl.when(z < n_z - 1)
    def _():
        greet(row + 2, col)

    for t in range(1, n_place):
        greet(row, lax.rem(place + t, n_place) * 2 + core)

    loads[0].wait()
    t_r, t_c = int_mask.shape
    h_r, h_c = raw.shape[0] // t_r, raw.shape[1] // t_c
    for i in range(t_r):
        for j in range(t_c):
            part = (slice(i * h_r, (i + 1) * h_r), slice(j * h_c, (j + 1) * h_c))
            keep = int_mask[i, j].astype(jnp.float32)
            ints[row, part[0], part[1]] = (raw[part].astype(jnp.float32) * keep).astype(ints.dtype)

    peers = n_place + 1 + (z > 0).astype(jnp.int32) + (z < n_z - 1).astype(jnp.int32)
    pl.semaphore_wait(barrier, peers)

    def move(r, send_sem, target):
        return pltpu.make_async_remote_copy(
            src_ref=ints.at[r], dst_ref=ints.at[r], send_sem=send_sem.at[r],
            recv_sem=ints_sem.at[r], device_id=(target, col), device_id_type=MESH,
        )

    def upward(r):
        return move(r, up_sem, row + 2)

    def downward(r):
        return move(r, down_sem, row - 2)

    def across(r):
        return move(r, across_sem, z * 2 + 1 - x)

    def pair_copy(step, q):
        return pltpu.make_async_remote_copy(
            src_ref=pair_out.at[step, q], dst_ref=pair_in.at[step, q],
            send_sem=pair_send.at[step, q], recv_sem=pair_recv.at[step, q],
            device_id=(row, place * 2 + 1 - core), device_id_type=MESH,
        )

    def far_copy(step, owner, h):
        return pltpu.make_async_remote_copy(
            src_ref=far_out.at[step, owner * pieces + h],
            dst_ref=far_in.at[step, place * pieces + h],
            send_sem=far_send.at[step, owner * pieces + h],
            recv_sem=far_recv.at[step, place * pieces + h],
            device_id=(row, owner * 2 + core), device_id_type=MESH,
        )

    def far_arrival(step, source, h):
        return pltpu.make_async_remote_copy(
            src_ref=far_out.at[step, source * pieces + h],
            dst_ref=far_in.at[step, source * pieces + h],
            send_sem=far_send.at[step, source * pieces + h],
            recv_sem=far_recv.at[step, source * pieces + h],
            device_id=(row, source * 2 + core), device_id_type=MESH,
        )

    def multiply(step, r):
        owner = r // pieces
        q = (owner // 2) * pieces + r % pieces
        mine = owner % 2 == core

        @pl.when(mine)
        def _():
            hold[q] = jnp.dot(masked[...], ints[r], preferred_element_type=jnp.float32)

        @pl.when(jnp.logical_not(mine))
        def _():
            pair_out[step, q] = jnp.dot(
                masked[...], ints[r], preferred_element_type=jnp.float32
            ).astype(pair_out.dtype)
            pair_copy(step, q).start()

    def combine(step, r):
        owner = r // pieces
        q = (owner // 2) * pieces + r % pieces

        @pl.when(owner % 2 == core)
        def _():
            pair_copy(step, q).wait_recv()

            @pl.when(owner // 2 == place)
            def _():
                hold[q] = hold[q] + pair_in[step, q].astype(jnp.float32)

            @pl.when(owner // 2 != place)
            def _():
                far_out[step, q] = (hold[q] + pair_in[step, q].astype(jnp.float32)).astype(far_out.dtype)
                far_copy(step, owner // 2, r % pieces).start()

    a_r, a_c = amp_mask.shape
    m_r, m_c = rows // a_r, amps.shape[1] // a_c

    def mask_amps():
        for i in range(a_r):
            for j in range(a_c):
                part = (slice(i * m_r, (i + 1) * m_r), slice(j * m_c, (j + 1) * m_c))
                keep = amp_mask[i, j].astype(jnp.float32)
                masked[part] = (amps[part].astype(jnp.float32) * keep).astype(masked.dtype)

    across(row).start()

    @pl.when(z < n_z - 1)
    def _():
        upward(row).start()

    @pl.when(z > 0)
    def _():
        downward(row).start()

    loads[1].wait()
    mask_amps()

    def each_side(distance, act):
        @pl.when((distance >= 0) & (z - distance >= 0))
        def _():
            act(z - distance, 1)

        @pl.when((distance > 0) & (z + distance < n_z))
        def _():
            act(z + distance, -1)

    def gather_step(d, _):
        def arrive(zz, direction):
            r = zz * 2 + x

            @pl.when(d > 0)
            def _():
                across(r).wait_recv()
                across(r).start()
                if direction > 0:
                    @pl.when(z < n_z - 1)
                    def _():
                        upward(r).start()
                else:
                    @pl.when(z > 0)
                    def _():
                        downward(r).start()

        def near(zz, direction):
            multiply(0, zz * 2 + x)

        def other(zz, direction):
            r = zz * 2 + 1 - x
            across(r).wait_recv()
            multiply(0, r)

        each_side(d, arrive)

        @pl.when(d < n_z)
        def _():
            each_side(d, near)

        each_side(d - 1, other)
        each_side(d - 1, lambda zz, direction: combine(0, zz * 2 + x))
        each_side(d - 2, lambda zz, direction: combine(0, zz * 2 + 1 - x))
        return 0

    lax.fori_loop(0, n_z + 2, gather_step, 0)

    loads[2].wait()
    loads[3].wait()
    r_r, r_c = res_mask.shape
    g_r, g_c = rows // r_r, amps.shape[1] // r_c

    def update(step):
        last = step == ITERS - 1
        stores = []
        for h in range(pieces):
            for t in range(1, n_place):
                far_arrival(step, lax.rem(place + t, n_place), h).wait_recv()
            for i in range(r_r):
                for j in range(h * width // g_c, (h + 1) * width // g_c):
                    down = slice(i * g_r, (i + 1) * g_r)
                    along = slice(j * g_c, (j + 1) * g_c)
                    local = slice(j * g_c - h * width, (j + 1) * g_c - h * width)
                    ladder = hold[place * pieces + h, down, local]
                    for t in range(1, n_place):
                        slot = lax.rem(place + t, n_place) * pieces + h
                        ladder = ladder + far_in[step, slot, down, local].astype(jnp.float32)
                    value = (base[down, along] + ladder) * res_mask[i, j].astype(jnp.float32)
                    if last:
                        res[down, along] = value
                    amps[down, along] = (
                        amps[down, along].astype(jnp.float32) - inv[down, along] * value
                    ).astype(amps.dtype)
            if last:
                cut = (slice(None), slice(h * width, (h + 1) * width))
                stores += [
                    pltpu.make_async_copy(amps.at[cut], new_hbm.at[cut], store_sem.at[2 * h]),
                    pltpu.make_async_copy(res.at[cut], res_hbm.at[cut], store_sem.at[2 * h + 1]),
                ]
                stores[-2].start()
                stores[-1].start()
        return stores

    stores = update(0)
    for step in range(1, ITERS):
        mask_amps()

        def place_step(t, _):
            there = lax.rem(place + 1 + t, n_place)
            first = there * 2 * pieces
            for h in range(pieces):
                multiply(step, first + (1 - core) * pieces + h)
            for h in range(pieces):
                multiply(step, first + core * pieces + h)
                combine(step, first + core * pieces + h)
            return 0

        lax.fori_loop(0, n_place, place_step, 0)
        stores = update(step)

    def drain_lines(zz, _):
        r = zz * 2 + x
        across(r).wait_send()

        @pl.when((zz <= z) & (z < n_z - 1))
        def _():
            upward(r).wait_send()

        @pl.when((zz >= z) & (z > 0))
        def _():
            downward(r).wait_send()

        return 0

    lax.fori_loop(0, n_z, drain_lines, 0)
    for step in range(ITERS):
        def drain_pair(q, _):
            pair_copy(step, q).wait_send()
            return 0

        lax.fori_loop(0, n_place * pieces, drain_pair, 0)
        for t in range(1, n_place):
            for h in range(pieces):
                far_copy(step, lax.rem(place + t, n_place), h).wait_send()
    for store in stores:
        store.wait()


def shards(n_row, n_col, amplitudes, integrals, base_residual, inv_denominators, amp_mask, int_mask, res_mask):
    rows, depth = amplitudes.shape
    width = integrals.shape[1]
    pieces = depth // width
    slots = (n_col // 2) * pieces
    any_spec = pl.BlockSpec(memory_space=pl.ANY)
    smem = pl.BlockSpec(memory_space=pltpu.SMEM)
    bf16, f32 = jnp.bfloat16, jnp.float32
    dma = pltpu.SemaphoreType.DMA
    return pl.pallas_call(
        functools.partial(kernel, n_row, n_col),
        out_shape=(
            jax.ShapeDtypeStruct(amplitudes.shape, bf16),
            jax.ShapeDtypeStruct(base_residual.shape, f32),
        ),
        in_specs=[smem] * 3 + [any_spec] * 4,
        out_specs=(any_spec, any_spec),
        scratch_shapes=[
            pltpu.VMEM(integrals.shape, bf16),
            pltpu.VMEM((n_row,) + integrals.shape, bf16),
            pltpu.VMEM((rows, depth), bf16),
            pltpu.VMEM((rows, depth), bf16),
            pltpu.VMEM((rows, depth), f32),
            pltpu.VMEM((rows, depth), f32),
            pltpu.VMEM((slots, rows, width), f32),
            pltpu.VMEM((ITERS, slots, rows, width), bf16),
            pltpu.VMEM((ITERS, slots, rows, width), bf16),
            pltpu.VMEM((ITERS, slots, rows, width), bf16),
            pltpu.VMEM((ITERS, slots, rows, width), bf16),
            pltpu.VMEM((rows, depth), f32),
            dma((4,)), dma((2 * pieces,)),
            dma((n_row,)), dma((n_row,)), dma((n_row,)), dma((n_row,)),
            dma((ITERS, slots)), dma((ITERS, slots)), dma((ITERS, slots)), dma((ITERS, slots)),
        ],
        compiler_params=pltpu.CompilerParams(
            collective_id=0, has_side_effects=True, vmem_limit_bytes=60 * 2**20
        ),
    )(amp_mask, int_mask, res_mask, amplitudes, integrals, base_residual, inv_denominators)


def solution(mesh):
    in_specs = (
        P("row", "col"),
        P("col", "row"),
        P("row", "col"),
        P("row", "col"),
        P("row", "col"),
        P("col", "row"),
        P("row", "col"),
    )
    out_specs = (P("row", "col"), P("row", "col"))
    body = functools.partial(shards, mesh.shape["row"], mesh.shape["col"])
    return jax.shard_map(body, mesh=mesh, in_specs=in_specs, out_specs=out_specs, check_vma=False)
```

time: 145 us -> 61.5 us (0.42)
  waiting for transfers between devices: 114 us -> 0 us
  Pallas kernels: 0 us -> 56.1 us
  between operations: 13.8 us -> 0.65 us
  other arithmetic: 7.79 us -> 0 us
  matrix products: 6.76 us -> 0 us
  local copies, waits for them, and re-layouts: 2.32 us -> 4.23 us
    reduce_scatter x2 -> x0, waiting for transfers between devices: 60.3 us -> none  [shards(): lax.psum_scatter(term.astype(jnp.bfloat16), 'col', scatter_dimension=1, t...]
    pallas_call x0 -> x1, Pallas kernels: none -> 56.1 us  [shards(): pl.pallas_call(functools.partial(kernel, n_row, n_col), out_shape=(jax.Sh...]
    all_gather x1 -> x0, waiting for transfers between devices: 53.4 us -> none  [shards(): ints_all = lax.all_gather(masked_ints, 'row', axis=1, tiled=True)]
    dot_general x2 -> x0, matrix products: 6.76 us -> none  [shards(): term = jnp.dot(masked_amps, ints_all, preferred_element_type=jnp.float32)]
    convert_element_type x5 -> x0, other arithmetic: 6.01 us -> none  [the longest x2 4.61 us: shards(): (amps.astype(jnp.float32) - inv_denominators * residual).astype(jnp.bfloa...]
    unnamed x20 -> x5, local copies, waits for them, and re-layouts: 1.64 us -> 4.23 us
    mul x1 -> x0, other arithmetic: 1.79 us -> none  [expand(): shaped * mask[:, None, :, None].astype(block.dtype)]
  transfers between devices with their start and end apart: 3 -> 0, of which waited for: 3 -> 0; matrix products, arithmetic and copies ran while one was open for 1% -> 0% of each run, Pallas kernels for 0% -> 0%
where the time goes in v1:
time: 61.5 us; the launch traced here: 61 us
  Pallas kernels  56.1 us (91%)
  local copies, waits for them, and re-layouts  4.23 us (7%)
  between operations  0.65 us (1%)
    pallas_call x1, Pallas kernels, shards(): pl.pallas_call(functools.partial(kernel, n_row, n_col), out_shape=(jax.Sh...  56.1 us
    unnamed x5, local copies, waits for them, and re-layouts  4.23 us

profile of v1, /device:TPU:0, one launch (start us, length us, event | category | flops | bytes accessed | tf_op | source)
XLA Modules:
  0.0 61.0 jit_solution(17178361506333760462)
XLA Ops:
  0.6 1.3 %copy.9.int_mask = s32[2,1]{1,0:T(2,128)} copy(s32[2,1]{0,1:T(1,128)} %param.12) | data formatting | bytes 16 | tf_op args[5]
  1.9 56.1 %shard_map.86 = (bf16[512,512]{1,0:T(8,128)(2,1)}, f32[512,512]{1,0:T(8,128)}) custom-call(s32[2,2]{1,0:T(2,128)} %amp_mask.1, s32[2,1]{1,0:T(2,128)} %copy.9.int_mask, s32[2,2]{1,0:T(2,128)} %res_mask.1, bf16[512,512]{1,0:T(8,128)(2,1)} %amps_hbm.1, bf16[512,256]{1,0:T(8,128)(2,1)} %ints_hbm.1, f32[512,512]{1,0:T(8,128)} %base_hbm.1, f32[512,512]{1,0:T(8,128)} %inv_hbm.1), custom_call_target="tpu_custom_call" | custom-call | tf_op jit(solution)/shard_map/pallas_call | solution.py:302
  58.1 0.0 copy-start
  58.1 2.0 %copy.12 = bf16[512,512]{1,0:T(8,128)(2,1)} copy(bf16[512,512]{1,0:T(8,128)(2,1)} %get-tuple-element.4) | data formatting | bytes 1048576
  60.0 0.0 copy-done
  60.0 1.0 %copy.13 = f32[512,512]{1,0:T(8,128)} copy(f32[512,512]{1,0:T(8,128)S(1)} %copy-done) | data formatting | bytes 2097152
Async XLA Ops:
  58.1 2.0 %copy-start = (f32[512,512]{1,0:T(8,128)S(1)}, f32[512,512]{1,0:T(8,128)}, u32[]{:S(2)}) copy-start(f32[512,512]{1,0:T(8,128)} %get-tuple-element.5) | copy-start | bytes 3145732

commit v2 on v1

--- a/solution.py
+++ b/solution.py
@@ -8,6 +8,7 @@
 from jax.sharding import PartitionSpec as P
 
 ITERS = 2
+CUTS = 2
 MESH = pl.DeviceIdType.MESH
 
 
@@ -55,13 +56,17 @@
         greet(row, lax.rem(place + t, n_place) * 2 + core)
 
     loads[0].wait()
-    t_r, t_c = int_mask.shape
+    t_c, t_r = int_mask.shape
     h_r, h_c = raw.shape[0] // t_r, raw.shape[1] // t_c
+    span = min(width, h_c)
     for i in range(t_r):
-        for j in range(t_c):
-            part = (slice(i * h_r, (i + 1) * h_r), slice(j * h_c, (j + 1) * h_c))
-            keep = int_mask[i, j].astype(jnp.float32)
-            ints[row, part[0], part[1]] = (raw[part].astype(jnp.float32) * keep).astype(ints.dtype)
+        for left in range(0, raw.shape[1], span):
+            down = slice(i * h_r, (i + 1) * h_r)
+            at = left % width
+            keep = int_mask[left // h_c, i].astype(jnp.float32)
+            ints[row * CUTS + left // width, down, at:at + span] = (
+                raw[down, left:left + span].astype(jnp.float32) * keep
+            ).astype(ints.dtype)
 
     peers = n_place + 1 + (z > 0).astype(jnp.int32) + (z < n_z - 1).astype(jnp.int32)
     pl.semaphore_wait(barrier, peers)
@@ -149,15 +154,16 @@
                 keep = amp_mask[i, j].astype(jnp.float32)
                 masked[part] = (amps[part].astype(jnp.float32) * keep).astype(masked.dtype)
 
-    across(row).start()
-
-    @pl.when(z < n_z - 1)
-    def _():
-        upward(row).start()
-
-    @pl.when(z > 0)
-    def _():
-        downward(row).start()
+    for s in range(CUTS):
+        across(row * CUTS + s).start()
+
+        @pl.when(z < n_z - 1)
+        def _():
+            upward(row * CUTS + s).start()
+
+        @pl.when(z > 0)
+        def _():
+            downward(row * CUTS + s).start()
 
     loads[1].wait()
     mask_amps()
@@ -173,28 +179,39 @@
 
     def gather_step(d, _):
         def arrive(zz, direction):
-            r = zz * 2 + x
-
             @pl.when(d > 0)
             def _():
+                for s in range(CUTS):
+                    r = (zz * 2 + x) * CUTS + s
+                    across(r).wait_recv()
+                    across(r).start()
+                    if direction > 0:
+                        @pl.when(z < n_z - 1)
+                        def _():
+                            upward(r).start()
+                    else:
+                        @pl.when(z > 0)
+                        def _():
+                            downward(r).start()
+
+        def near(zz, direction):
+            for s in range(CUTS):
+                multiply(0, (zz * 2 + x) * CUTS + s)
+
+        def other(zz, direction):
+            for s in range(CUTS):
+                r = (zz * 2 + 1 - x) * CUTS + s
                 across(r).wait_recv()
-                across(r).start()
-                if direction > 0:
-                    @pl.when(z < n_z - 1)
-                    def _():
-                        upward(r).start()
-                else:
-                    @pl.when(z > 0)
-                    def _():
-                        downward(r).start()
-
-        def near(zz, direction):
-            multiply(0, zz * 2 + x)
-
-        def other(zz, direction):
-            r = zz * 2 + 1 - x
-            across(r).wait_recv()
-            multiply(0, r)
+                multiply(0, r)
+                if s > 0:
+                    combine(0, r - 1)
+
+        def near_sum(zz, direction):
+            for s in range(CUTS):
+                combine(0, (zz * 2 + x) * CUTS + s)
+
+        def other_sum(zz, direction):
+            combine(0, (zz * 2 + 1 - x) * CUTS + CUTS - 1)
 
         each_side(d, arrive)
 
@@ -202,9 +219,9 @@
         def _():
             each_side(d, near)
 
+        each_side(d - 1, near_sum)
         each_side(d - 1, other)
-        each_side(d - 1, lambda zz, direction: combine(0, zz * 2 + x))
-        each_side(d - 2, lambda zz, direction: combine(0, zz * 2 + 1 - x))
+        each_side(d - 2, other_sum)
         return 0
 
     lax.fori_loop(0, n_z + 2, gather_step, 0)
@@ -220,16 +237,18 @@
         for h in range(pieces):
             for t in range(1, n_place):
                 far_arrival(step, lax.rem(place + t, n_place), h).wait_recv()
+            span = min(width, g_c)
             for i in range(r_r):
-                for j in range(h * width // g_c, (h + 1) * width // g_c):
+                for at in range(0, width, span):
                     down = slice(i * g_r, (i + 1) * g_r)
-                    along = slice(j * g_c, (j + 1) * g_c)
-                    local = slice(j * g_c - h * width, (j + 1) * g_c - h * width)
+                    along = slice(h * width + at, h * width + at + span)
+                    local = slice(at, at + span)
+                    keep = res_mask[i, (h * width + at) // g_c].astype(jnp.float32)
                     ladder = hold[place * pieces + h, down, local]
                     for t in range(1, n_place):
                         slot = lax.rem(place + t, n_place) * pieces + h
                         ladder = ladder + far_in[step, slot, down, local].astype(jnp.float32)
-                    value = (base[down, along] + ladder) * res_mask[i, j].astype(jnp.float32)
+                    value = (base[down, along] + ladder) * keep
                     if last:
                         res[down, along] = value
                     amps[down, along] = (
@@ -254,25 +273,27 @@
             first = there * 2 * pieces
             for h in range(pieces):
                 multiply(step, first + (1 - core) * pieces + h)
-            for h in range(pieces):
                 multiply(step, first + core * pieces + h)
-                combine(step, first + core * pieces + h)
+                if h > 0:
+                    combine(step, first + core * pieces + h - 1)
+            combine(step, first + core * pieces + pieces - 1)
             return 0
 
         lax.fori_loop(0, n_place, place_step, 0)
         stores = update(step)
 
     def drain_lines(zz, _):
-        r = zz * 2 + x
-        across(r).wait_send()
-
-        @pl.when((zz <= z) & (z < n_z - 1))
-        def _():
-            upward(r).wait_send()
-
-        @pl.when((zz >= z) & (z > 0))
-        def _():
-            downward(r).wait_send()
+        for s in range(CUTS):
+            r = (zz * 2 + x) * CUTS + s
+            across(r).wait_send()
+
+            @pl.when((zz <= z) & (z < n_z - 1))
+            def _():
+                upward(r).wait_send()
+
+            @pl.when((zz >= z) & (z > 0))
+            def _():
+                downward(r).wait_send()
 
         return 0
 
@@ -292,7 +313,8 @@
 
 def shards(n_row, n_col, amplitudes, integrals, base_residual, inv_denominators, amp_mask, int_mask, res_mask):
     rows, depth = amplitudes.shape
-    width = integrals.shape[1]
+    width = integrals.shape[1] // CUTS
+    blocks = n_row * CUTS
     pieces = depth // width
     slots = (n_col // 2) * pieces
     any_spec = pl.BlockSpec(memory_space=pl.ANY)
@@ -309,7 +331,7 @@
         out_specs=(any_spec, any_spec),
         scratch_shapes=[
             pltpu.VMEM(integrals.shape, bf16),
-            pltpu.VMEM((n_row,) + integrals.shape, bf16),
+            pltpu.VMEM((blocks, integrals.shape[0], width), bf16),
             pltpu.VMEM((rows, depth), bf16),
             pltpu.VMEM((rows, depth), bf16),
             pltpu.VMEM((rows, depth), f32),
@@ -321,13 +343,13 @@
             pltpu.VMEM((ITERS, slots, rows, width), bf16),
             pltpu.VMEM((rows, depth), f32),
             dma((4,)), dma((2 * pieces,)),
-            dma((n_row,)), dma((n_row,)), dma((n_row,)), dma((n_row,)),
+            dma((blocks,)), dma((blocks,)), dma((blocks,)), dma((blocks,)),
             dma((ITERS, slots)), dma((ITERS, slots)), dma((ITERS, slots)), dma((ITERS, slots)),
         ],
         compiler_params=pltpu.CompilerParams(
             collective_id=0, has_side_effects=True, vmem_limit_bytes=60 * 2**20
         ),
-    )(amp_mask, int_mask, res_mask, amplitudes, integrals, base_residual, inv_denominators)
+    )(amp_mask, int_mask.T, res_mask, amplitudes, integrals, base_residual, inv_denominators)
 
 
 def solution(mesh):

time: 61.5 us -> 58.3 us (0.948)
  Pallas kernels: 56.1 us -> 54.5 us
  local copies, waits for them, and re-layouts: 4.23 us -> 2.93 us
    pallas_call x1, Pallas kernels: 56.1 us -> 54.5 us  [shards(): pl.pallas_call(functools.partial(kernel, n_row, n_col), out_shape=(jax.Sh...]
    unnamed x5 -> x4, local copies, waits for them, and re-layouts: 4.23 us -> 2.93 us
where the time goes in v2:
time: 58.3 us; the launch traced here: 58.1 us
  Pallas kernels  54.5 us (93%)
  local copies, waits for them, and re-layouts  2.93 us (5%)
  between operations  0.65 us (1%)
    pallas_call x1, Pallas kernels, shards(): pl.pallas_call(functools.partial(kernel, n_row, n_col), out_shape=(jax.Sh...  54.5 us
    unnamed x4, local copies, waits for them, and re-layouts  2.93 us

profile of v2, /device:TPU:0, one launch (start us, length us, event | category | flops | bytes accessed | tf_op | source)
XLA Modules:
  0.0 58.1 jit_solution(6418911548607976522)
XLA Ops:
  0.6 54.5 %shard_map.86 = (bf16[512,512]{1,0:T(8,128)(2,1)}, f32[512,512]{1,0:T(8,128)}) custom-call(s32[2,2]{1,0:T(2,128)} %amp_mask.1, s32[1,2]{1,0:T(1,128)} %bitcast.1, s32[2,2]{1,0:T(2,128)} %res_mask.1, bf16[512,512]{1,0:T(8,128)(2,1)} %amps_hbm.1, bf16[512,256]{1,0:T(8,128)(2,1)} %ints_hbm.1, f32[512,512]{1,0:T(8,128)} %base_hbm.1, f32[512,512]{1,0:T(8,128)} %inv_hbm.1), custom_call_target="tpu_custom_call" | custom-call | tf_op jit(solution)/shard_map/pallas_call | solution.py:324
  55.2 0.0 copy-start
  55.2 2.0 %copy.11 = bf16[512,512]{1,0:T(8,128)(2,1)} copy(bf16[512,512]{1,0:T(8,128)(2,1)} %get-tuple-element.4) | data formatting | bytes 1048576
  57.1 0.0 copy-done
  57.1 1.0 %copy.12 = f32[512,512]{1,0:T(8,128)} copy(f32[512,512]{1,0:T(8,128)S(1)} %copy-done) | data formatting | bytes 2097152
Async XLA Ops:
  55.2 2.0 %copy-start = (f32[512,512]{1,0:T(8,128)S(1)}, f32[512,512]{1,0:T(8,128)}, u32[]{:S(2)}) copy-start(f32[512,512]{1,0:T(8,128)} %get-tuple-element.5) | copy-start | bytes 3145732

commit v3 on v2

--- a/solution.py
+++ b/solution.py
@@ -218,13 +218,13 @@
         @pl.when(d < n_z)
         def _():
             each_side(d, near)
-
-        each_side(d - 1, near_sum)
+            each_side(d, near_sum)
+
         each_side(d - 1, other)
-        each_side(d - 2, other_sum)
+        each_side(d - 1, other_sum)
         return 0
 
-    lax.fori_loop(0, n_z + 2, gather_step, 0)
+    lax.fori_loop(0, n_z + 1, gather_step, 0)
 
     loads[2].wait()
     loads[3].wait()

time: 58.3 us -> 56.3 us (0.966)
  Pallas kernels: 54.5 us -> 52.5 us
    pallas_call x1, Pallas kernels: 54.5 us -> 52.5 us  [shards(): pl.pallas_call(functools.partial(kernel, n_row, n_col), out_shape=(jax.Sh...]
where the time goes in v3:
time: 56.3 us; the launch traced here: 56.1 us
  Pallas kernels  52.5 us (93%)
  local copies, waits for them, and re-layouts  2.93 us (5%)
  between operations  0.65 us (1%)
    pallas_call x1, Pallas kernels, shards(): pl.pallas_call(functools.partial(kernel, n_row, n_col), out_shape=(jax.Sh...  52.5 us
    unnamed x4, local copies, waits for them, and re-layouts  2.93 us

profile of v3, /device:TPU:0, one launch (start us, length us, event | category | flops | bytes accessed | tf_op | source)
XLA Modules:
  0.0 56.1 jit_solution(6826381402668786649)
XLA Ops:
  0.6 52.5 %shard_map.86 = (bf16[512,512]{1,0:T(8,128)(2,1)}, f32[512,512]{1,0:T(8,128)}) custom-call(s32[2,2]{1,0:T(2,128)} %amp_mask.1, s32[1,2]{1,0:T(1,128)} %bitcast.1, s32[2,2]{1,0:T(2,128)} %res_mask.1, bf16[512,512]{1,0:T(8,128)(2,1)} %amps_hbm.1, bf16[512,256]{1,0:T(8,128)(2,1)} %ints_hbm.1, f32[512,512]{1,0:T(8,128)} %base_hbm.1, f32[512,512]{1,0:T(8,128)} %inv_hbm.1), custom_call_target="tpu_custom_call" | custom-call | tf_op jit(solution)/shard_map/pallas_call | solution.py:324
  53.2 0.0 copy-start
  53.2 2.0 %copy.11 = bf16[512,512]{1,0:T(8,128)(2,1)} copy(bf16[512,512]{1,0:T(8,128)(2,1)} %get-tuple-element.4) | data formatting | bytes 1048576
  55.1 0.0 copy-done
  55.1 1.0 %copy.12 = f32[512,512]{1,0:T(8,128)} copy(f32[512,512]{1,0:T(8,128)S(1)} %copy-done) | data formatting | bytes 2097152
Async XLA Ops:
  53.2 2.0 %copy-start = (f32[512,512]{1,0:T(8,128)S(1)}, f32[512,512]{1,0:T(8,128)}, u32[]{:S(2)}) copy-start(f32[512,512]{1,0:T(8,128)} %get-tuple-element.5) | copy-start | bytes 3145732
